TPU v7x, 128 devices: a whole 4x4x4 slice. The times are simulated.
128 devices in a mesh: dom: 8 (over z, core), tile: 16 (over y, x).
Axes of the slice: x: 4, y: 4, z: 4, core: 2. Of those that a mesh axis runs over, the one named last changes fastest.
Arguments:
- images: bfloat16 [512, 256, 256], P('dom', 'tile'), may hold values from -26 to 26
- defocus: float32 [512], P('dom'), may hold values from 0.5 to 3
- noise_weight: float32 [256, 128], P('tile'), may hold values from 0.5 to 4
- references: bfloat16 [2048, 256, 256], P(None, 'tile'), may hold values from -5 to 5
- candidates: int32 [512, 2], P('dom'), may hold values from 0 to 2047, as said below
- route: int32 [8, 16, 64, 2, 16], P('dom', 'tile'), may hold values from 0 to 127, as said below
- strips: int32 [8, 16, 64, 2, 16], P('dom', 'tile'), may hold values from 0 to 2047
Outputs:
- backprojection: float32 [262144, 384], P(('dom', 'tile'))
- spread: float32 [512], P('dom')
Inputs may be any that keep to these rules, and one draw needn't show every extreme that they name: `candidates`: the 2 references of a particle differ. `route`: of the rows of one device, every owner receives either none or exactly 32; one owner, the same for all devices, receives 32 rows from every device.
All inputs are finite; a program needn't handle non-finite values.
Results may differ from a plain program's by a relative error of at most 0.005.
Values may be sent and summed in bfloat16 or wider, within the bound.
A program may use at most 128 MiB of HBM per device.

v0:
```python
import math

import jax
import jax.numpy as jnp
from jax import lax
from jax.sharding import PartitionSpec as P

STRIPS = 2048


CONTRAST_SCALE = 400.0
PHASE_SHIFT = 0.1


def contrast_table(defocus, row_start, row_count, all_rows, half_width):
    row_ids = row_start + jnp.arange(row_count, dtype=jnp.int32)
    row_freq = jnp.where(row_ids < all_rows // 2, row_ids, row_ids - all_rows).astype(jnp.float32)
    col_freq = jnp.arange(half_width, dtype=jnp.int32).astype(jnp.float32)
    radius = (
        row_freq[:, None] * row_freq[:, None] + col_freq[None, :] * col_freq[None, :]
    ) / float(all_rows * all_rows)
    return -jnp.sin(CONTRAST_SCALE * defocus[:, None, None] * radius[None] + PHASE_SHIFT)


def shards(images, defocus, noise_weight, references, candidates, route, strips):
    tile_count = lax.axis_size("tile")
    dom_count = lax.axis_size("dom")
    device_count = dom_count * tile_count
    particle_count = images.shape[0]
    row_count = images.shape[1]
    half_width = noise_weight.shape[1]
    ref_count = references.shape[0]
    all_rows = row_count * tile_count
    tile_pos = lax.axis_index("tile")
    contrast = contrast_table(defocus, tile_pos * row_count, row_count, all_rows, half_width)
    contrast_pair = jnp.concatenate([contrast, contrast], axis=2)
    weight_pair = jnp.concatenate([noise_weight, noise_weight], axis=1)
    weighted = (contrast_pair * weight_pair[None] * images.astype(jnp.float32)).astype(jnp.bfloat16)
    power_map = (contrast * contrast * noise_weight[None]).astype(jnp.bfloat16)
    ref_values = references.astype(jnp.float32)
    squares = (
        ref_values[:, :, :half_width] * ref_values[:, :, :half_width]
        + ref_values[:, :, half_width:] * ref_values[:, :, half_width:]
    ).astype(jnp.bfloat16)
    contract_dims = (((1,), (1,)), ((), ()))
    crossed = lax.dot_general(
        weighted.reshape(particle_count, -1),
        references.reshape(ref_count, -1),
        contract_dims,
        preferred_element_type=jnp.float32,
    )
    energy = lax.dot_general(
        power_map.reshape(particle_count, -1),
        squares.reshape(ref_count, -1),
        contract_dims,
        preferred_element_type=jnp.float32,
    )
    score_scale = 1.0 / math.sqrt(all_rows * half_width)
    partial_value = (crossed - 0.5 * energy) * score_scale
    scores = lax.psum(partial_value, "tile")
    highest = jnp.max(scores, axis=1, keepdims=True)
    spread = jnp.log(jnp.sum(jnp.exp(scores - highest), axis=1))
    matches = candidates[:, :, None] == jnp.arange(ref_count, dtype=jnp.int32)[None, None, :]
    picked = jnp.sum(jnp.where(matches, scores[:, None, :], 0.0), axis=2)
    best_pick = jnp.max(picked, axis=1, keepdims=True)
    raised = jnp.exp(picked - best_pick)
    chosen = raised / jnp.sum(raised, axis=1, keepdims=True)
    owners = route.reshape(-1)
    strip_ids = strips.reshape(-1)
    flat_count = owners.shape[0]
    capacity = 2 * flat_count // device_count
    sort_order = jnp.argsort(owners, stable=True)
    sorted_owner = owners[sort_order]
    counts = jnp.sum(
        (owners[:, None] == jnp.arange(device_count, dtype=jnp.int32)[None, :]).astype(jnp.int32),
        axis=0,
    )
    starts = jnp.cumsum(counts) - counts
    position = jnp.arange(flat_count, dtype=jnp.int32) - starts[sorted_owner]
    slot_index = sorted_owner * capacity + position
    slot_total = device_count * capacity
    joined = jnp.concatenate([weighted, power_map], axis=2).astype(jnp.float32)
    rows_out = (chosen[:, :, None, None] * joined[:, None]).astype(jnp.bfloat16)
    flat_rows = rows_out.reshape(-1, 3 * half_width)
    send_rows = (
        jnp.zeros((slot_total, 3 * half_width), jnp.bfloat16)
        .at[slot_index]
        .set(flat_rows[sort_order])
    )
    send_strips = jnp.zeros((slot_total,), jnp.int32).at[slot_index].set(strip_ids[sort_order])
    got_rows, got_strips = (
        lax.all_to_all(
            send_rows.reshape(device_count, capacity, 3 * half_width),
            ("dom", "tile"),
            split_axis=0,
            concat_axis=0,
            tiled=True,
        ),
        lax.all_to_all(
            send_strips.reshape(device_count, capacity),
            ("dom", "tile"),
            split_axis=0,
            concat_axis=0,
            tiled=True,
        ),
    )
    final_rows = got_rows.reshape(-1, 3 * half_width).astype(jnp.float32)
    final_strips = got_strips.reshape(-1)
    volume = jnp.zeros((STRIPS, 3 * half_width), jnp.float32)
    volume = volume.at[final_strips].add(final_rows)
    return (volume, spread)


def solution(mesh):
    in_specs = (
        P("dom", "tile", None),
        P("dom"),
        P("tile", None),
        P(None, "tile", None),
        P("dom", None),
        P("dom", "tile", None, None, None),
        P("dom", "tile", None, None, None),
    )
    out_specs = (P(("dom", "tile"), None), P("dom"))
    return jax.shard_map(shards, mesh=mesh, in_specs=in_specs, out_specs=out_specs, check_vma=False)
```

profile of v0, /device:TPU:1, one launch (start us, length us, event | category | flops | bytes accessed | tf_op | source)
XLA Modules:
  0.0 257.9 jit_solution(1062703238247258833)
XLA Ops:
  7.2 0.7 broadcast_multiply_fusion
  7.9 0.8 pad_maximum_fusion
  8.7 18.9 %convert_element_type.57 = f32[2048,16,256]{2,1,0:T(8,128)} convert(bf16[2048,16,256]{2,1,0:T(8,128)(2,1)} %param.10) | non-fusion elementwise | flops 8388608 | bytes 50331648 | tf_op jit(solution)/shard_map/convert_element_type | solution.py:40
  27.7 1.9 fusion.31
  29.5 0.1 fusion.29
  29.7 19.4 %fusion.12 = f32[64,2048]{1,0:T(8,128)S(1)} fusion(bf16[2048,16,256]{2,1,0:T(8,128)(2,1)} %param.10, bf16[64,16,256]{2,1,0:T(8,128)(2,1)S(1)} %fusion.29), kind=kOutput, calls=%fused_computation.20 | convolution fusion | flops 1073741824 | bytes 17825792 | tf_op jit(solution)/shard_map/dot_general | solution.py:46
  49.1 11.6 %fusion.1 = bf16[2048,16,128]{2,1,0:T(8,128)(2,1)S(1)} fusion(f32[2048,16,256]{2,1,0:T(8,128)} %convert_element_type.57), kind=kLoop, calls=%fused_computation.9 | loop fusion | flops 16777216 | bytes 41943040 | tf_op jit(solution)/shard_map/convert_element_type | solution.py:44
  60.8 3.5 %fusion.21 = f32[64,2048]{1,0:T(8,128)} fusion(f32[64,2048]{1,0:T(8,128)S(1)} %fusion.12, bf16[2048,16,128]{2,1,0:T(8,128)(2,1)S(1)} %fusion.1, bf16[64,16,128]{2,1,0:T(8,128)(2,1)S(1)} %get-tuple-element.5), kind=kOutput, calls=%fused_computation.23 | convolution fusion | flops 537264128 | bytes 9699328 | tf_op jit(solution)/shard_map/dot_general | solution.py:52
  64.4 0.1 reshape.228
  64.5 0.4 convert_reduce_fusion
  64.9 5.0 %sort.17 = (s32[2048]{0:T(1024)}, s32[2048]{0:T(1024)S(1)}) sort(s32[2048]{0:T(1024)S(1)} %reshape.228, s32[2048]{0:T(1024)S(1)} %iota.26), dimensions={0}, to_apply=%region_0.1 | sort | flops 22528 | bytes 32768 | tf_op jit(solution)/shard_map/jit(argsort)/sort | solution.py:72
  69.9 11.8 %gather_fusion = s32[2048]{0:T(1024)S(1)} fusion(s32[2048]{0:T(1024)S(1)} %reshape.228, s32[2048]{0:T(1024)S(1)} %fusion.33), kind=kCustom, calls=%fused_computation | custom fusion | bytes 24576 | tf_op jit(solution)/shard_map/gather | solution.py:73
  81.8 0.2 reduce-window.9
  82.4 11.8 %gather_fusion.2 = s32[2048]{0:T(1024)S(1)} fusion(s32[2048]{0:T(1024)S(1)} %reshape.231, s32[2048]{0:T(1024)S(1)} %fusion.33), kind=kCustom, calls=%fused_computation.2 | custom fusion | bytes 24576 | tf_op jit(solution)/shard_map/gather | solution.py:90
  94.2 12.6 %gather_fusion.1 = s32[2048]{0:T(1024)S(1)} fusion(s32[128]{0:T(128)S(1)} %sub.39, s32[2048]{0:T(1024)S(1)} %broadcast_clamp_fusion), kind=kCustom, calls=%fused_computation.1 | custom fusion | bytes 24576 | tf_op jit(solution)/shard_map/gather | solution.py:79
  106.8 8.1 %scatter_custom_fusion = s32[4096]{0:T(1024)S(1)} fusion(s32[2048]{0:T(1024)S(1)} %bitcast.30, s32[2048]{0:T(1024)S(1)} %gather_fusion.2, s32[]{:T(128)} %constant.17.clone.1), kind=kCustom, calls=%fused_computation.49 | custom fusion | bytes 16388 | tf_op jit(solution)/shard_map/scatter | solution.py:90
  114.9 0.7 all_to_all.9
  115.6 11.5 %all-to-all-start = ((s32[128,1,32]{2,1,0:T(1,128)}), s32[128,1,32]{2,1,0:T(1,128)S(1)}, u32[]{:S(2)}, u32[]{:S(2)}) async-start(s32[128,1,32]{2,1,0:T(1,128)} %bitcast.5), calls=%async_computation | async-start | bytes 131072 | tf_op jit(solution)/shard_map/all_to_all | solution.py:99
  127.2 24.1 %all-reduce.2.cloned.1.call-done = f32[64,2048]{1,0:T(8,128)} async-done(((f32[64,2048]{1,0:T(8,128)}), f32[64,2048]{1,0:T(8,128)}) %all-reduce.2.cloned.1.call-update) | async-done | bytes 524304 | tf_op jit(solution)/shard_map/psum | solution.py:60
  151.3 1.3 select_reduce_fusion
  152.7 0.1 mul.140
  152.9 0.1 mul.141
  153.0 0.3 fusion.8
  153.4 19.2 %scatter_custom_fusion.1 = bf16[4096,384]{1,0:T(8,128)(2,1)} fusion(s32[2048]{0:T(1024)S(1)} %bitcast.31, bf16[2048,384]{1,0:T(8,128)(2,1)S(1)} %fusion.8, s32[2048]{0:T(1024)S(1)} %fusion.33, bf16[]{:T(256)} %constant.22.clone.1), kind=kCustom, calls=%fused_computation.24 | custom fusion | bytes 3145730 | tf_op jit(solution)/shard_map/scatter | solution.py:88
  172.5 9.0 %all-to-all-start.1 = ((bf16[128,32,384]{2,1,0:T(8,128)(2,1)}), bf16[128,32,384]{2,1,0:T(8,128)(2,1)S(1)}, u32[]{:S(2)}, u32[]{:S(2)}) async-start(bf16[128,32,384]{2,1,0:T(8,128)(2,1)} %bitcast.10), calls=%async_computation.1 | async-start | bytes 6291456 | tf_op jit(solution)/shard_map/all_to_all | solution.py:92
  181.5 0.5 broadcast.183
  182.1 0.8 reduce.4
  183.0 1.2 reduce_max.19
  184.2 1.3 exponential_reduce_fusion
  185.5 0.5 log.3
  186.0 36.4 %all-to-all-done.1 = bf16[128,32,384]{2,1,0:T(8,128)(2,1)S(1)} async-done(((bf16[128,32,384]{2,1,0:T(8,128)(2,1)}), bf16[128,32,384]{2,1,0:T(8,128)(2,1)S(1)}, u32[]{:S(2)}, u32[]{:S(2)}) %all-to-all-start.1) | async-done | bytes 3145760 | tf_op jit(solution)/shard_map/all_to_all | solution.py:92
  222.5 28.6 %scatter_custom_fusion.2 = f32[2048,384]{1,0:T(8,128)} fusion(s32[4096]{0:T(1024)S(1)} %bitcast.29, bf16[4096,384]{1,0:T(8,128)(2,1)S(1)} %bitcast.24, f32[]{:T(128)} %constant.16.clone.1), kind=kCustom, calls=%fused_computation.15 | custom fusion | flops 3145728 | bytes 6291460 | tf_op jit(solution)/shard_map/scatter-add | solution.py:110
  (34 shorter events, 1.1 us)
Async XLA Ops:
  7.2 144.1 %all-reduce.2.cloned.1.call-start = ((), (), s32[]{:S(2)}) async-start(), calls=%async_computation.2 | async-start | bytes 1048576 | tf_op jit(solution)/shard_map/psum | solution.py:60
  8.7 19.0 %copy-start.1 = (f32[16,128]{1,0:T(8,128)S(1)}, f32[16,128]{1,0:T(8,128)}, u32[]{:S(2)}) copy-start(f32[16,128]{1,0:T(8,128)} %param.9) | copy-start | bytes 24580
  8.7 20.9 %copy-start = (bf16[64,16,256]{2,1,0:T(8,128)(2,1)S(1)}, bf16[64,16,256]{2,1,0:T(8,128)(2,1)}, u32[]{:S(2)}) copy-start(bf16[64,16,256]{2,1,0:T(8,128)(2,1)} %param.7) | copy-start | bytes 1572868
  60.7 3.5 %copy-start.2 = (s32[1,1,64,2,16]{2,4,3,1,0:T(8,128)S(1)}, s32[1,1,64,2,16]{2,4,3,1,0:T(8,128)}, u32[]{:S(2)}) copy-start(s32[1,1,64,2,16]{2,4,3,1,0:T(8,128)} %param.12) | copy-start | bytes 24580
  69.9 12.2 %copy-start.3 = (s32[1,1,64,2,16]{2,4,3,1,0:T(8,128)S(1)}, s32[1,1,64,2,16]{2,4,3,1,0:T(8,128)}, u32[]{:S(2)}) copy-start(s32[1,1,64,2,16]{2,4,3,1,0:T(8,128)} %param.13) | copy-start | bytes 24580
  94.1 57.1 %copy-start.4 = (s32[64,2]{0,1:T(2,128)S(1)}, s32[64,2]{0,1:T(2,128)}, u32[]{:S(2)}) copy-start(s32[64,2]{0,1:T(2,128)} %param.11) | copy-start | bytes 1540
  115.6 57.0 %all-to-all-start = ((s32[128,1,32]{2,1,0:T(1,128)}), s32[128,1,32]{2,1,0:T(1,128)S(1)}, u32[]{:S(2)}, u32[]{:S(2)}) async-start(s32[128,1,32]{2,1,0:T(1,128)} %bitcast.5), calls=%async_computation | async-start | bytes 131072 | tf_op jit(solution)/shard_map/all_to_all | solution.py:99
  172.5 49.9 %all-to-all-start.1 = ((bf16[128,32,384]{2,1,0:T(8,128)(2,1)}), bf16[128,32,384]{2,1,0:T(8,128)(2,1)S(1)}, u32[]{:S(2)}, u32[]{:S(2)}) async-start(bf16[128,32,384]{2,1,0:T(8,128)(2,1)} %bitcast.10), calls=%async_computation.1 | async-start | bytes 6291456 | tf_op jit(solution)/shard_map/all_to_all | solution.py:92
Sparse Core Ops, SparseCore 0:
  64.4 86.8 all-reduce.1
where the time goes:
time: 258 us
  other arithmetic  73.4 us (28%)
  local copies, waits for them, and re-layouts  66.2 us (26%)
  waiting for transfers between devices  60.5 us (23%)
  matrix products  22.9 us (9%)
  starting transfers between devices  20.5 us (8%)
  between operations  14.3 us (6%)
    all_to_all x1, waiting for transfers between devices, shards(): lax.all_to_all(send_rows.reshape(device_count, capacity, 3 * half_width),...  36.4 us
    scatter-add x1, other arithmetic, shards(): volume = volume.at[final_strips].add(final_rows)  28.6 us
    psum x1, waiting for transfers between devices, shards(): scores = lax.psum(partial_value, 'tile')  24.1 us
    dot_general x1, matrix products, shards(): lax.dot_general(weighted.reshape(particle_count, -1), references.reshape(...  19.4 us
    scatter x1, local copies, waits for them, and re-layouts, shards(): send_rows = jnp.zeros((slot_total, 3 * half_width), jnp.bfloat16).at[slot...  19.2 us
    convert_element_type x1, other arithmetic, shards(): ref_values = references.astype(jnp.float32)  18.9 us
    gather x1, local copies, waits for them, and re-layouts, shards(): position = jnp.arange(flat_count, dtype=jnp.int32) - starts[sorted_owner]  12.6 us
    gather x1, local copies, waits for them, and re-layouts, shards(): strip_ids[sort_order]  11.8 us
  transfers between devices with their start and end apart: 3, of which 2 were waited for; matrix products, arithmetic and copies ran while one was open for 30% of the time, Pallas kernels for 0%

commit v1 on v0

v1 whole, which is shorter than its diff:
```python
import math

import jax
import jax.numpy as jnp
from jax import lax
from jax.experimental import pallas as pl
from jax.experimental.pallas import tpu as pltpu
from jax.sharding import PartitionSpec as P

F32 = jnp.float32
BF16 = jnp.bfloat16
I32 = jnp.int32
MESH = pl.DeviceIdType.MESH
NT = (((1,), (1,)), ((), ()))

STRIPS = 2048
HALF = 128
ROWS_DEV = 16
PD = 64
MINE = PD * ROWS_DEV
NREF = 2048
REFS = NREF // 2
WIDE = 3 * HALF
DEPTH = ROWS_DEV * WIDE
CHUNK = 256

TURN = 400.0 / 65536.0 / (2.0 * math.pi)
PHASE = 0.1 / (2.0 * math.pi)
SCALE = 1.0 / math.sqrt(32768.0)
SERIES = (
    6.283182793407029,
    -41.34141938561706,
    81.59613875538182,
    -76.5796878510169,
    41.20374363365668,
    -12.268859941003917,
)


def wave(turns):
    frac = turns - jnp.floor(turns + 0.5)
    sq = frac * frac
    total = jnp.full_like(sq, SERIES[-1])
    for coef in SERIES[-2::-1]:
        total = total * sq + coef
    return total * frac


def iota(shape, dim):
    return lax.broadcasted_iota(I32, shape, dim)


def kernel(
    img_ref, focus_ref, info_ref, noise_ref, refs_ref, owner_ref, strip_ref,
    vol_ref, spread_ref,
    rv, xc, xw, wi, pmo, ot, rank_ref, mask_ref, sb, rb, meta0, meta1, meta2,
    info, noise, score, part, stats, picks, stack, table, low, high, code, weight, pm,
    ref_sem, data_send, data_recv, xw_sem, info_sem, noise_sem, m1_sem, m2_sem, part_sem, stat_sem, pick_sem,
):
    dom = lax.axis_index("dom")
    tile = lax.axis_index("tile")
    core = lax.rem(dom, 2)
    barrier = pltpu.get_barrier_semaphore()

    def loads(c):
        return pltpu.make_async_copy(
            refs_ref.at[pl.ds(core * REFS + c * CHUNK, CHUNK)],
            rv.at[pl.ds(c * CHUNK, CHUNK)],
            ref_sem.at[c],
        )

    for c in range(REFS // CHUNK):
        loads(c).start()

    def greet(s, carry):
        pl.semaphore_signal(
            barrier,
            inc=1,
            device_id=(jnp.bitwise_xor(dom, s // 16), jnp.bitwise_xor(tile, lax.rem(s, 16))),
            device_id_type=MESH,
        )
        return carry

    lax.fori_loop(1, 128, greet, 0)

    def remote(src, dst, sems, d, t):
        return pltpu.make_async_remote_copy(
            src_ref=src, dst_ref=dst, send_sem=sems[0], recv_sem=sems[1],
            device_id=(d, t), device_id_type=MESH,
        )

    def pair(sem):
        return sem.at[0], sem.at[1]

    def wait_for(ref, sem):
        pltpu.make_async_copy(ref, ref, sem).wait()

    def freq_sq(rows):
        return jnp.where(rows < 128, rows, rows - 256).astype(F32)

    def weigh(c, carry):
        row_f = freq_sq(tile * 16 + iota((8, 16, HALF), 1))
        col_f = iota((8, 16, HALF), 2).astype(F32)
        radius = row_f * row_f + col_f * col_f
        focus = focus_ref[pl.ds(c * 8, 8)]
        contrast = -wave(focus * TURN * radius + PHASE)
        noise_here = noise_ref[...][None]
        power = (contrast * contrast * noise_here).astype(BF16)
        gain = contrast * noise_here
        start = pl.multiple_of(c * 128, 128)
        pmo[pl.ds(start, 128), :] = power.reshape(128, HALF)
        rows = img_ref[pl.ds(start, 128), :].astype(F32)
        gain = gain.reshape(128, HALF)
        wi[pl.ds(start, 128), 0:HALF] = (gain * rows[:, :HALF]).astype(BF16)
        wi[pl.ds(start, 128), HALF:] = (gain * rows[:, HALF:]).astype(BF16)
        return carry

    lax.fori_loop(0, 8, weigh, 0)

    ia, ib = iota((256, 256), 0), iota((256, 256), 1)
    swap = jnp.where(((ia & 15) * 16 + (ia >> 4)) == ib, 1.0, 0.0).astype(BF16)
    for b in range(4):
        at = pl.multiple_of(core * PD + b * 16, 16)
        left = jnp.dot(swap, wi[b * 256:(b + 1) * 256, :], preferred_element_type=F32).astype(BF16)
        right = (-0.5 * jnp.dot(swap, pmo[b * 256:(b + 1) * 256, :], preferred_element_type=F32)).astype(BF16)
        for i in range(16):
            xw[pl.ds(at, 16), i * WIDE:i * WIDE + 256] = left[i * 16:(i + 1) * 16]
            xw[pl.ds(at, 16), i * WIDE + 256:(i + 1) * WIDE] = right[i * 16:(i + 1) * 16]

    upper = jnp.where(ia < ib, 1.0, 0.0).astype(BF16)
    running = jnp.zeros((128, 1), F32)
    meta_low = jnp.zeros((128, 128), F32)
    meta_high = jnp.zeros((128, 128), F32)
    owner_id = iota((128, 256), 0)
    for k in range(2):
        for b in range(4):
            cols = slice(b * 256, (b + 1) * 256)
            owner = owner_ref[k:k + 1, cols]
            owner = ((owner & 15) << 3) | (owner >> 4)
            hit = jnp.where(owner_id == owner, 1.0, 0.0)
            hit16 = hit.astype(BF16)
            before = jnp.dot(hit16, upper, preferred_element_type=F32) + running
            rank = jnp.sum(hit * before, axis=0, keepdims=True)
            running = running + jnp.sum(hit, axis=1, keepdims=True)
            for t in range(16):
                ot[k, t, :, cols] = hit[t * 8:(t + 1) * 8]
            rank_ref[k:k + 1, cols] = rank
            strip = strip_ref[k:k + 1, cols] + 1
            number = iota((1, 256), 1) + b * 256
            group = owner_id >> 5
            same = (owner_id & 31).astype(F32) == rank
            low_value = jnp.where(group < 2, strip & 255, number & 255).astype(F32)
            high_value = jnp.where(group < 2, strip >> 8, (number >> 8) + 4 * k).astype(F32)
            low16 = jnp.where(same, low_value, 0.0).astype(BF16)
            high16 = jnp.where(same, high_value, 0.0).astype(BF16)
            meta_low = meta_low + lax.dot_general(hit16, low16, NT, preferred_element_type=F32)
            meta_high = meta_high + lax.dot_general(hit16, high16, NT, preferred_element_type=F32)
    meta = meta_low + 256.0 * meta_high
    for t in range(16):
        for d in range(8):
            meta0[t, d] = meta[t * 8 + d:t * 8 + d + 1, :]
    slot_id = iota((32, MINE), 0).astype(F32)
    for k in range(2):
        mask_ref[k] = jnp.where(slot_id == rank_ref[k:k + 1, :], 1.0, 0.0).astype(BF16)

    pl.semaphore_wait(barrier, 127)
    mate = jnp.bitwise_xor(dom, 1)
    mine = pl.ds(pl.multiple_of(core * PD, PD), PD)
    other = pl.ds(pl.multiple_of((1 - core) * PD, PD), PD)
    remote(xw.at[mine], xw.at[mine], pair(xw_sem), mate, tile).start()
    meta1[0] = meta0[tile]
    info[0] = info_ref[...]
    noise[0] = noise_ref[...]

    def small(u, carry):
        t = jnp.bitwise_xor(tile, u)
        remote(meta0.at[t], meta1.at[u], pair(m1_sem), dom, t).start()
        remote(noise_ref, noise.at[u], pair(noise_sem), dom, t).start()
        return carry

    lax.fori_loop(1, 16, small, 0)

    def small_dom(e, carry):
        remote(info_ref, info.at[e], pair(info_sem), jnp.bitwise_xor(dom, e), tile).start()
        return carry

    lax.fori_loop(1, 8, small_dom, 0)

    def pack(u):
        t = jnp.bitwise_xor(tile, u)
        blocks = []
        for d in range(8):
            one = ot[0, t, d:d + 1, :].astype(BF16)
            two = ot[1, t, d:d + 1, :].astype(BF16)
            blocks.append(mask_ref[0] * one + mask_ref[1] * two)
        rows = jnp.dot(jnp.concatenate(blocks, axis=0), wi[...], preferred_element_type=F32).astype(BF16)
        for d in range(8):
            sb[u, d] = rows[d * 32:(d + 1) * 32]
        return t

    def ship(u, e, t):
        d = jnp.bitwise_xor(dom, e)
        remote(sb.at[u, d], rb.at[u, e], (data_send, data_recv.at[u]), d, t).start()

    def rows_of(i, carry):
        u = lax.rem(i * 7, 16)
        t = pack(u)
        for e in range(8):
            ship(u, e, t)
        return carry

    lax.fori_loop(1, 16, rows_of, 0)
    here = pack(0)
    for e in range(1, 8):
        ship(0, e, here)
    rb[0, 0] = sb[0, dom]

    wait_for(meta1.at[pl.ds(1, 15)], m1_sem.at[1])
    for u in range(16):
        meta2[0, u] = meta1[u, dom]

    def forward(e, carry):
        d = jnp.bitwise_xor(dom, e)
        remote(meta1.at[:, d], meta2.at[e], pair(m2_sem), d, tile).start()
        return carry

    lax.fori_loop(1, 8, forward, 0)

    wait_for(xw.at[other], xw_sem.at[1])
    row = tile // 4
    column = lax.rem(tile, 4)
    for c in range(REFS // CHUNK):
        loads(c).wait()

    def scored(i, carry):
        chunk = jnp.bitwise_xor(row, lax.rem(i + 1, 4))
        base = pl.multiple_of(chunk * CHUNK, CHUNK)

        def block(b, inner):
            refs = rv[pl.ds(base + b * 16, 16)].reshape(256, 256)
            turned = jnp.dot(swap, refs, preferred_element_type=F32)
            squares = (turned[:, :HALF] * turned[:, :HALF] + turned[:, HALF:] * turned[:, HALF:]).astype(BF16)
            turned = turned.astype(BF16)
            at = pl.multiple_of(b * 16, 16)
            for r in range(16):
                xc[pl.ds(at, 16), r * WIDE:r * WIDE + 256] = turned[r * 16:(r + 1) * 16]
                xc[pl.ds(at, 16), r * WIDE + 256:(r + 1) * WIDE] = squares[r * 16:(r + 1) * 16]
            return inner

        lax.fori_loop(0, CHUNK // 16, block, 0)
        score[pl.ds(base, CHUNK), :] = SCALE * lax.dot_general(xc[...], xw[...], NT, preferred_element_type=F32)

        def share(v, inner):
            t = chunk * 4 + jnp.bitwise_xor(column, v)
            u = jnp.bitwise_xor(t, tile)

            @pl.when(u != 0)
            def _():
                remote(score.at[pl.ds(pl.multiple_of(t * 64, 64), 64)], part.at[u], pair(part_sem), dom, t).start()

            return inner

        lax.fori_loop(0, 4, share, 0)
        return carry

    lax.fori_loop(0, 4, scored, 0)
    part[0] = score[pl.ds(pl.multiple_of(tile * 64, 64), 64), :]

    wait_for(info.at[pl.ds(1, 7)], info_sem.at[1])
    wait_for(noise.at[pl.ds(1, 15)], noise_sem.at[1])
    wait_for(meta2.at[pl.ds(1, 7)], m2_sem.at[1])
    lane1 = iota((1, HALF), 1)
    stack[...] = jnp.zeros_like(stack)
    for w in range(4):
        focus = jnp.where(lane1 < PD, info[2 * w, 2:3, :], info[2 * w + 1, 2:3, :])
        first = focus.astype(BF16).astype(F32)
        second = (focus - first).astype(BF16).astype(F32)
        stack[4 * w:4 * w + 1, :] = first
        stack[4 * w + 1:4 * w + 2, :] = second
        stack[4 * w + 2:4 * w + 3, :] = focus - first - second
    focus_rows = stack[...].astype(BF16)
    lane2 = iota((1, 256), 1)

    def prepare(u, carry):
        quarter = lane1 >> 5
        strips, numbers = [], []
        for half in range(2):
            strip = jnp.zeros((1, HALF), F32)
            number = jnp.zeros((1, HALF), F32)
            for a in range(4):
                got = meta2[half * 4 + a, u]
                back = pltpu.roll(got, 64, 1)
                strip = jnp.where(quarter == a, got if a < 2 else back, strip)
                number = jnp.where(quarter == a, back if a < 2 else got, number)
            strips.append(strip)
            numbers.append(number)
        strip = jnp.concatenate(strips, axis=1).astype(I32) - 1
        number = jnp.concatenate(numbers, axis=1).astype(I32)
        low[u] = (strip & 255).astype(F32)
        high[u] = (strip >> 8).astype(F32)
        r = number & 15
        particle = ((number >> 4) & 63) + 64 * ((lane2 >> 5) & 1)
        code[u] = (particle + 128 * (number >> 10)).astype(F32)
        hot = jnp.where(iota((HALF, 256), 0) == particle, 1.0, 0.0).astype(BF16)
        found = jnp.dot(focus_rows, hot, preferred_element_type=F32)
        found = jnp.where((iota((16, 256), 0) >> 2) == (lane2 >> 6), found, 0.0)
        slope = jnp.sum(found, axis=0, keepdims=True) * TURN
        row_f = freq_sq(jnp.bitwise_xor(tile, u) * 16 + r)
        offset = slope * (row_f * row_f) + PHASE
        which = iota((8, 256), 0)
        rows = jnp.where(which == 0, slope, jnp.where(which == 1, offset, r.astype(F32)))
        turned = jnp.transpose(rows)
        col_f = iota((256, HALF), 1).astype(F32)
        contrast = wave(turned[:, 0:1] * (col_f * col_f) + turned[:, 1:2])
        pick_row = jnp.where((iota((256, 48), 1) & 15).astype(F32) == turned[:, 2:3], 1.0, 0.0).astype(BF16)
        full = noise[u]
        first = full.astype(BF16)
        second = (full - first.astype(F32)).astype(BF16)
        third = (full - first.astype(F32) - second.astype(F32)).astype(BF16)
        gain = jnp.dot(pick_row, jnp.concatenate([first, second, third], axis=0), preferred_element_type=F32)
        pm[u] = (contrast * contrast * gain).astype(BF16)
        return carry

    lax.fori_loop(0, 8, prepare, 0)

    wait_for(part.at[pl.ds(1, 15)], part_sem.at[1])
    total = part[0]
    for u in range(1, 16):
        total = total + part[u]
    same_core = jnp.where(core == 0, 0, 1)
    cand = []
    for k in range(2):
        zero = info[same_core, k:k + 1, :]
        one = info[1 - same_core, k:k + 1, :]
        cand.append(jnp.where(lane1 < PD, zero, one))
    ids = (iota((64, HALF), 0) + core * REFS + tile * 64).astype(F32)
    top = jnp.max(total, axis=0, keepdims=True)
    mass = jnp.sum(jnp.exp(total - top), axis=0, keepdims=True)
    got0 = jnp.sum(jnp.where(ids == cand[0], total, 0.0), axis=0, keepdims=True)
    got1 = jnp.sum(jnp.where(ids == cand[1], total, 0.0), axis=0, keepdims=True)
    which = iota((8, HALF), 0)
    stats[0] = jnp.where(which == 0, top, jnp.where(which == 1, mass, jnp.where(which == 2, got0, got1)))

    def tell(v, carry):
        d = jnp.bitwise_xor(dom, v // 16)
        t = jnp.bitwise_xor(tile, lax.rem(v, 16))
        remote(stats.at[0], stats.at[v], pair(stat_sem), d, t).start()
        return carry

    lax.fori_loop(1, 32, tell, 0)
    lax.fori_loop(8, 12, prepare, 0)
    wait_for(stats.at[pl.ds(1, 31)], stat_sem.at[1])
    every = stats[...]
    tops = every[:, 0, :]
    top = jnp.max(tops, axis=0, keepdims=True)
    mass = jnp.sum(every[:, 1, :] * jnp.exp(tops - top), axis=0, keepdims=True)
    got0 = jnp.sum(every[:, 2, :], axis=0, keepdims=True)
    got1 = jnp.sum(every[:, 3, :], axis=0, keepdims=True)
    spread = jnp.log(mass)
    best = jnp.maximum(got0, got1)
    raised0 = jnp.exp(got0 - best)
    raised1 = jnp.exp(got1 - best)
    chosen0 = raised0 / (raised0 + raised1)
    chosen1 = raised1 / (raised0 + raised1)
    rows = jnp.where(which == 0, chosen0, jnp.where(which == 1, chosen1, spread))
    rows = jnp.where(core == 0, rows, pltpu.roll(rows, 64, 1))
    picks[0] = rows
    spread_ref[...] = rows

    def pass_on(w, carry):
        remote(picks.at[0], picks.at[w], pair(pick_sem), jnp.bitwise_xor(dom, 2 * w), tile).start()
        return carry

    lax.fori_loop(1, 4, pass_on, 0)
    lax.fori_loop(12, 16, prepare, 0)
    wait_for(picks.at[pl.ds(1, 3)], pick_sem.at[1])
    for w in range(4):
        table[2 * w:2 * w + 2, :] = picks[w, 0:2, :]
    chosen_rows = table[...].astype(BF16)

    def choose(u, carry):
        number = code[u].astype(I32)
        hot = jnp.where(iota((HALF, 256), 0) == (number & 127), 1.0, 0.0).astype(BF16)
        found = jnp.dot(chosen_rows, hot, preferred_element_type=F32)
        keep = iota((8, 256), 0) == ((lane2 >> 6) * 2 + (number >> 7))
        weight[u] = jnp.sum(jnp.where(keep, found, 0.0), axis=0, keepdims=True)
        return carry

    lax.fori_loop(0, 16, choose, 0)

    order = [(i * 7) % 16 for i in range(1, 16)]
    del order
    slab_row = iota((256, 4 * 256), 0).astype(F32).astype(BF16)
    for g in range(4):
        for u in range(4 * g, 4 * g + 4):
            if u == 0:
                wait_for(rb.at[0, pl.ds(0, 7)], data_recv.at[0])
            else:
                wait_for(rb.at[u], data_recv.at[u])
        low16 = jnp.concatenate([low[u] for u in range(4 * g, 4 * g + 4)], axis=1).astype(BF16)
        high_row = jnp.concatenate([high[u] for u in range(4 * g, 4 * g + 4)], axis=1)
        share_row = jnp.concatenate([weight[u] for u in range(4 * g, 4 * g + 4)], axis=1)

        def insert(b, carry):
            value = jnp.where(high_row == b.astype(F32), share_row, 0.0).astype(BF16)
            spot = jnp.where(slab_row == low16, value, jnp.zeros_like(value))
            rows = rb[4 * g:4 * g + 4].reshape(1024, 256)
            power = pm[4 * g:4 * g + 4].reshape(1024, HALF)
            at = pl.ds(pl.multiple_of(b * 256, 256), 256)
            data = jnp.dot(spot, rows, preferred_element_type=F32)
            more = jnp.dot(spot, power, preferred_element_type=F32)
            if g == 0:
                vol_ref[at, 0:256] = data
                vol_ref[at, 256:] = more
            else:
                vol_ref[at, 0:256] += data
                vol_ref[at, 256:] += more
            return carry

        lax.fori_loop(0, 8, insert, 0)

    wait_for(xw.at[mine], xw_sem.at[0])
    wait_for(meta1.at[pl.ds(1, 15)], m1_sem.at[0])
    wait_for(noise.at[pl.ds(1, 15)], noise_sem.at[0])
    wait_for(info.at[pl.ds(1, 7)], info_sem.at[0])
    wait_for(meta2.at[pl.ds(1, 7)], m2_sem.at[0])
    wait_for(part.at[pl.ds(1, 15)], part_sem.at[0])
    wait_for(stats.at[pl.ds(1, 31)], stat_sem.at[0])
    wait_for(picks.at[pl.ds(1, 3)], pick_sem.at[0])
    wait_for(sb.at[pl.ds(1, 15)], data_send)
    wait_for(sb.at[0, pl.ds(0, 7)], data_send)


def shards(images, defocus, noise_weight, references, candidates, route, strips):
    rows = images.reshape(MINE, 2 * HALF)
    focus = jnp.broadcast_to(defocus[:, None, None], (PD, 1, HALF))
    cand = jnp.transpose(candidates).astype(F32)
    short = jnp.concatenate([cand, defocus[None], jnp.zeros((5, PD), F32)], axis=0)
    info = jnp.concatenate([short, short], axis=1)
    owners = jnp.transpose(route[0, 0], (1, 0, 2)).reshape(2, MINE)
    places = jnp.transpose(strips[0, 0], (1, 0, 2)).reshape(2, MINE)
    vmem = pl.BlockSpec(memory_space=pltpu.VMEM)
    dma = pltpu.SemaphoreType.DMA
    volume, spread = pl.pallas_call(
        kernel,
        out_shape=(
            jax.ShapeDtypeStruct((STRIPS, WIDE), F32),
            jax.ShapeDtypeStruct((8, HALF), F32),
        ),
        in_specs=[vmem, vmem, vmem, vmem, pl.BlockSpec(memory_space=pl.ANY), vmem, vmem],
        out_specs=(vmem, vmem),
        scratch_shapes=[
            pltpu.VMEM((REFS, ROWS_DEV, 2 * HALF), BF16),
            pltpu.VMEM((CHUNK, DEPTH), BF16),
            pltpu.VMEM((2 * PD, DEPTH), BF16),
            pltpu.VMEM((MINE, 2 * HALF), BF16),
            pltpu.VMEM((MINE, HALF), BF16),
            pltpu.VMEM((2, 16, 8, MINE), F32),
            pltpu.VMEM((2, MINE), F32),
            pltpu.VMEM((2, 32, MINE), BF16),
            pltpu.VMEM((16, 8, 32, 256), BF16),
            pltpu.VMEM((16, 8, 32, 256), BF16),
            pltpu.VMEM((16, 8, 1, HALF), F32),
            pltpu.VMEM((16, 8, 1, HALF), F32),
            pltpu.VMEM((8, 16, 1, HALF), F32),
            pltpu.VMEM((8, 8, HALF), F32),
            pltpu.VMEM((16, 16, HALF), F32),
            pltpu.VMEM((REFS, 2 * PD), F32),
            pltpu.VMEM((16, 64, 2 * PD), F32),
            pltpu.VMEM((32, 8, HALF), F32),
            pltpu.VMEM((4, 8, HALF), F32),
            pltpu.VMEM((16, HALF), F32),
            pltpu.VMEM((8, HALF), F32),
            pltpu.VMEM((16, 1, 256), F32),
            pltpu.VMEM((16, 1, 256), F32),
            pltpu.VMEM((16, 1, 256), F32),
            pltpu.VMEM((16, 1, 256), F32),
            pltpu.VMEM((16, 256, HALF), BF16),
            dma((REFS // CHUNK,)),
            dma,
            dma((16,)),
        ] + [dma((2,))] * 8,
        compiler_params=pltpu.CompilerParams(
            collective_id=0, has_side_effects=True, vmem_limit_bytes=56 << 20
        ),
    )(rows, focus, info, noise_weight, references, owners, places)
    return volume, spread[2, :PD]


def solution(mesh):
    in_specs = (
        P("dom", "tile", None),
        P("dom"),
        P("tile", None),
        P(None, "tile", None),
        P("dom", None),
        P("dom", "tile", None, None, None),
        P("dom", "tile", None, None, None),
    )
    out_specs = (P(("dom", "tile"), None), P("dom"))
    return jax.shard_map(shards, mesh=mesh, in_specs=in_specs, out_specs=out_specs, check_vma=False)
```

time: 258 us -> 91.3 us (0.35)
  Pallas kernels: 0 us -> 78.9 us
  other arithmetic: 73.4 us -> 2.08 us
  waiting for transfers between devices: 60.5 us -> 0 us
  local copies, waits for them, and re-layouts: 66.2 us -> 9.33 us
  matrix products: 22.9 us -> 0 us
  starting transfers between devices: 20.5 us -> 0 us
  between operations: 14.3 us -> 0.64 us
    pallas_call x0 -> x1, Pallas kernels: none -> 78.9 us  [shards(): pl.pallas_call(kernel, out_shape=(jax.ShapeDtypeStruct((STRIPS, WIDE), F3...]
    all_to_all x2 -> x0, waiting for transfers between devices: 36.4 us -> none  [the longest x1 36.4 us: shards(): lax.all_to_all(send_rows.reshape(device_count, capacity, 3 * half_width),...]
    gather x3 -> x0, local copies, waits for them, and re-layouts: 36.2 us -> none  [the longest x1 12.6 us: shards(): position = jnp.arange(flat_count, dtype=jnp.int32) - starts[sorted_owner]]
    convert_element_type x5 -> x1, other arithmetic: 31.1 us -> 0.68 us  [shards(): cand = jnp.transpose(candidates).astype(F32)]
    scatter-add x1 -> x0, other arithmetic: 28.6 us -> none  [shards(): volume = volume.at[final_strips].add(final_rows)]
    scatter x2 -> x0, local copies, waits for them, and re-layouts: 27.2 us -> none  [the longest x1 19.2 us: shards(): send_rows = jnp.zeros((slot_total, 3 * half_width), jnp.bfloat16).at[slot...]
    psum x1 -> x0, waiting for transfers between devices: 24.1 us -> none  [shards(): scores = lax.psum(partial_value, 'tile')]
    dot_general x2 -> x0, matrix products: 22.9 us -> none  [the longest x1 19.4 us: shards(): lax.dot_general(weighted.reshape(particle_count, -1), references.reshape(...]
  transfers between devices with their start and end apart: 3 -> 0, of which waited for: 2 -> 0; matrix products, arithmetic and copies ran while one was open for 30% -> 0% of each run, Pallas kernels for 0% -> 0%
where the time goes in v1:
time: 91.3 us; the launch traced here: 90.9 us
  Pallas kernels  78.9 us (86%)
  local copies, waits for them, and re-layouts  9.33 us (10%)
  other arithmetic  2.08 us (2%)
    pallas_call x1, Pallas kernels, shards(): pl.pallas_call(kernel, out_shape=(jax.ShapeDtypeStruct((STRIPS, WIDE), F3...  78.9 us
    unnamed x1, local copies, waits for them, and re-layouts  3.75 us

profile of v1, /device:TPU:1, one launch (start us, length us, event | category | flops | bytes accessed | tf_op | source)
XLA Modules:
  0.0 90.9 jit_solution(1675731456272530470)
XLA Ops:
  0.6 0.7 convert_bitcast_fusion
  1.3 1.4 %maximum_maximum_fusion.info_ref = f32[8,128]{1,0:T(8,128)} fusion(f32[5,64]{1,0:T(8,128)S(1)} %broadcast_in_dim.14, f32[1,64]{1,0:T(1,128)} %bitcast.15, f32[2,64]{1,0:T(2,128)S(1)} %convert_bitcast_fusion), kind=kLoop, calls=%fused_computation | loop fusion | flops 5120 | bytes 6144 | tf_op jit(solution)/shard_map/concatenate | solution.py:439
  2.7 1.4 %broadcast_in_dim.12.focus_ref = f32[64,1,128]{2,1,0:T(1,128)} broadcast(f32[64]{0:T(128)} %param.8), dimensions={0} | broadcast | bytes 33024 | tf_op jit(solution)/shard_map/broadcast_in_dim | solution.py:436
  4.1 0.8 copy.11
  4.9 0.7 reshape.17.owner_ref
  5.6 0.8 copy.12
  6.4 0.7 reshape.18.strip_ref
  7.1 78.9 %shard_map.86 = (f32[2048,384]{1,0:T(8,128)}, f32[8,128]{1,0:T(8,128)}) custom-call(bf16[1024,256]{1,0:T(8,128)(2,1)} %bitcast.12, f32[64,1,128]{2,1,0:T(1,128)} %broadcast_in_dim.12.focus_ref, f32[8,128]{1,0:T(8,128)} %maximum_maximum_fusion.info_ref, f32[16,128]{1,0:T(8,128)} %noise_ref.1, bf16[2048,16,256]{2,1,0:T(8,128)(2,1)} %refs_ref.1, ...), custom_call_target="tpu_custom_call" | custom-call | tf_op jit(solution)/shard_map/pallas_call | solution.py:444
  86.0 1.2 %slice_bitcast_fusion = f32[64]{0:T(128)} fusion(f32[8,128]{1,0:T(8,128)} %get-tuple-element.5), kind=kLoop, calls=%fused_computation.2 | loop fusion | bytes 512 | tf_op jit(solution)/shard_map/squeeze | solution.py:487
  87.2 3.8 %copy.14 = f32[2048,384]{1,0:T(8,128)} copy(f32[2048,384]{1,0:T(8,128)} %get-tuple-element.8) | data formatting | bytes 6291456
  (1 shorter events, 0.0 us)

commit v2 on v1

--- a/solution.py
+++ b/solution.py
@@ -23,6 +23,8 @@
 WIDE = 3 * HALF
 DEPTH = ROWS_DEV * WIDE
 CHUNK = 256
+EARLY = 8
+FIRST, SECOND, THIRD = 8, 11, 14
 
 TURN = 400.0 / 65536.0 / (2.0 * math.pi)
 PHASE = 0.1 / (2.0 * math.pi)
@@ -51,11 +53,11 @@
 
 
 def kernel(
-    img_ref, focus_ref, info_ref, noise_ref, refs_ref, owner_ref, strip_ref,
+    img_ref, focus_ref, cand_ref, noise_ref, refs_ref, route_ref, place_ref,
     vol_ref, spread_ref,
     rv, xc, xw, wi, pmo, ot, rank_ref, mask_ref, sb, rb, meta0, meta1, meta2,
-    info, noise, score, part, stats, picks, stack, table, low, high, code, weight, pm,
-    ref_sem, data_send, data_recv, xw_sem, info_sem, noise_sem, m1_sem, m2_sem, part_sem, stat_sem, pick_sem,
+    lanes, info, noise, score, part, stats, picks, stack, table, low, high, code, weight, pm,
+    ref_sem, data_send, data_recv, all_sem, xw_sem, info_sem, noise_sem, m1_sem, m2_sem, part_sem, stat_sem, pick_sem,
 ):
     dom = lax.axis_index("dom")
     tile = lax.axis_index("tile")
@@ -72,16 +74,20 @@
     for c in range(REFS // CHUNK):
         loads(c).start()
 
-    def greet(s, carry):
-        pl.semaphore_signal(
-            barrier,
-            inc=1,
-            device_id=(jnp.bitwise_xor(dom, s // 16), jnp.bitwise_xor(tile, lax.rem(s, 16))),
-            device_id_type=MESH,
-        )
-        return carry
-
-    lax.fori_loop(1, 128, greet, 0)
+    def greet_tile(u, carry):
+        pl.semaphore_signal(barrier, inc=1, device_id=(dom, jnp.bitwise_xor(tile, u)), device_id_type=MESH)
+        return carry
+
+    def greet_dom(e, carry):
+        pl.semaphore_signal(barrier, inc=1, device_id=(jnp.bitwise_xor(dom, e), tile), device_id_type=MESH)
+        return carry
+
+    def vouch(e, carry):
+        pl.semaphore_signal(all_sem, inc=1, device_id=(jnp.bitwise_xor(dom, e), tile), device_id_type=MESH)
+        return carry
+
+    lax.fori_loop(1, 16, greet_tile, 0)
+    lax.fori_loop(1, 8, greet_dom, 0)
 
     def remote(src, dst, sems, d, t):
         return pltpu.make_async_remote_copy(
@@ -95,22 +101,42 @@
     def wait_for(ref, sem):
         pltpu.make_async_copy(ref, ref, sem).wait()
 
+    info[0] = jnp.zeros((8, HALF), F32)
+    for k in range(2):
+        cand_row = cand_ref[k:k + 1, :].astype(F32)
+        info[0, k:k + 1, :] = jnp.concatenate([cand_row, cand_row], axis=1)
+    info[0, 2:3, :] = jnp.concatenate([focus_ref[...], focus_ref[...]], axis=1)
+    widen = jnp.where((iota((PD, MINE), 1) >> 4) == iota((PD, MINE), 0), 1.0, 0.0).astype(BF16)
+    diagonal = (iota((16, MINE), 1) & 15) == iota((16, MINE), 0)
+
+    def along(block):
+        wide = jnp.dot(block.astype(F32).astype(BF16), widen, preferred_element_type=F32)
+        return jnp.sum(jnp.where(diagonal, wide, 0.0), axis=0, keepdims=True)
+
+    for k in range(2):
+        lanes[k:k + 1, :] = along(route_ref[k])
+        place = place_ref[k] + 1
+        lanes[2 + k:3 + k, :] = along(place & 255)
+        lanes[4 + k:5 + k, :] = along(place >> 8)
+
     def freq_sq(rows):
         return jnp.where(rows < 128, rows, rows - 256).astype(F32)
 
+    focus_row = info[0, 2:3, :]
+
     def weigh(c, carry):
-        row_f = freq_sq(tile * 16 + iota((8, 16, HALF), 1))
-        col_f = iota((8, 16, HALF), 2).astype(F32)
+        row = iota((128, HALF), 0)
+        lane = iota((128, HALF), 1)
+        row_f = freq_sq(tile * 16 + (row & 15))
+        col_f = lane.astype(F32)
         radius = row_f * row_f + col_f * col_f
-        focus = focus_ref[pl.ds(c * 8, 8)]
+        focus = jnp.sum(jnp.where(lane == c * 8 + (row >> 4), focus_row, 0.0), axis=1, keepdims=True)
         contrast = -wave(focus * TURN * radius + PHASE)
-        noise_here = noise_ref[...][None]
-        power = (contrast * contrast * noise_here).astype(BF16)
+        noise_here = jnp.concatenate([noise_ref[...]] * 8, axis=0)
+        start = pl.multiple_of(c * 128, 128)
+        pmo[pl.ds(start, 128), :] = (contrast * contrast * noise_here).astype(BF16)
         gain = contrast * noise_here
-        start = pl.multiple_of(c * 128, 128)
-        pmo[pl.ds(start, 128), :] = power.reshape(128, HALF)
         rows = img_ref[pl.ds(start, 128), :].astype(F32)
-        gain = gain.reshape(128, HALF)
         wi[pl.ds(start, 128), 0:HALF] = (gain * rows[:, :HALF]).astype(BF16)
         wi[pl.ds(start, 128), HALF:] = (gain * rows[:, HALF:]).astype(BF16)
         return carry
@@ -135,7 +161,7 @@
     for k in range(2):
         for b in range(4):
             cols = slice(b * 256, (b + 1) * 256)
-            owner = owner_ref[k:k + 1, cols]
+            owner = lanes[k:k + 1, cols].astype(I32)
             owner = ((owner & 15) << 3) | (owner >> 4)
             hit = jnp.where(owner_id == owner, 1.0, 0.0)
             hit16 = hit.astype(BF16)
@@ -145,12 +171,11 @@
             for t in range(16):
                 ot[k, t, :, cols] = hit[t * 8:(t + 1) * 8]
             rank_ref[k:k + 1, cols] = rank
-            strip = strip_ref[k:k + 1, cols] + 1
             number = iota((1, 256), 1) + b * 256
             group = owner_id >> 5
             same = (owner_id & 31).astype(F32) == rank
-            low_value = jnp.where(group < 2, strip & 255, number & 255).astype(F32)
-            high_value = jnp.where(group < 2, strip >> 8, (number >> 8) + 4 * k).astype(F32)
+            low_value = jnp.where(group < 2, lanes[2 + k:3 + k, cols], (number & 255).astype(F32))
+            high_value = jnp.where(group < 2, lanes[4 + k:5 + k, cols], ((number >> 8) + 4 * k).astype(F32))
             low16 = jnp.where(same, low_value, 0.0).astype(BF16)
             high16 = jnp.where(same, high_value, 0.0).astype(BF16)
             meta_low = meta_low + lax.dot_general(hit16, low16, NT, preferred_element_type=F32)
@@ -163,31 +188,11 @@
     for k in range(2):
         mask_ref[k] = jnp.where(slot_id == rank_ref[k:k + 1, :], 1.0, 0.0).astype(BF16)
 
-    pl.semaphore_wait(barrier, 127)
-    mate = jnp.bitwise_xor(dom, 1)
-    mine = pl.ds(pl.multiple_of(core * PD, PD), PD)
-    other = pl.ds(pl.multiple_of((1 - core) * PD, PD), PD)
-    remote(xw.at[mine], xw.at[mine], pair(xw_sem), mate, tile).start()
-    meta1[0] = meta0[tile]
-    info[0] = info_ref[...]
-    noise[0] = noise_ref[...]
-
-    def small(u, carry):
-        t = jnp.bitwise_xor(tile, u)
-        remote(meta0.at[t], meta1.at[u], pair(m1_sem), dom, t).start()
-        remote(noise_ref, noise.at[u], pair(noise_sem), dom, t).start()
-        return carry
-
-    lax.fori_loop(1, 16, small, 0)
-
-    def small_dom(e, carry):
-        remote(info_ref, info.at[e], pair(info_sem), jnp.bitwise_xor(dom, e), tile).start()
-        return carry
-
-    lax.fori_loop(1, 8, small_dom, 0)
-
-    def pack(u):
-        t = jnp.bitwise_xor(tile, u)
+    def turn_of(i):
+        return lax.rem(7 * (i + 1), 16)
+
+    def pack(i, carry):
+        t = jnp.bitwise_xor(tile, turn_of(i))
         blocks = []
         for d in range(8):
             one = ot[0, t, d:d + 1, :].astype(BF16)
@@ -195,25 +200,46 @@
             blocks.append(mask_ref[0] * one + mask_ref[1] * two)
         rows = jnp.dot(jnp.concatenate(blocks, axis=0), wi[...], preferred_element_type=F32).astype(BF16)
         for d in range(8):
-            sb[u, d] = rows[d * 32:(d + 1) * 32]
-        return t
-
-    def ship(u, e, t):
-        d = jnp.bitwise_xor(dom, e)
-        remote(sb.at[u, d], rb.at[u, e], (data_send, data_recv.at[u]), d, t).start()
-
-    def rows_of(i, carry):
-        u = lax.rem(i * 7, 16)
-        t = pack(u)
+            sb[i, d] = rows[d * 32:(d + 1) * 32]
+        return carry
+
+    lax.fori_loop(0, EARLY, pack, 0)
+
+    pl.semaphore_wait(barrier, 22)
+    lax.fori_loop(1, 8, vouch, 0)
+    mate = jnp.bitwise_xor(dom, 1)
+    mine = pl.ds(pl.multiple_of(core * PD, PD), PD)
+    other = pl.ds(pl.multiple_of((1 - core) * PD, PD), PD)
+    remote(xw.at[mine], xw.at[mine], pair(xw_sem), mate, tile).start()
+    meta1[0] = meta0[tile]
+    noise[0] = noise_ref[...]
+
+    def small(u, carry):
+        t = jnp.bitwise_xor(tile, u)
+        remote(meta0.at[t], meta1.at[u], pair(m1_sem), dom, t).start()
+        remote(noise_ref, noise.at[u], pair(noise_sem), dom, t).start()
+        return carry
+
+    lax.fori_loop(1, 16, small, 0)
+
+    def small_dom(e, carry):
+        remote(info.at[0], info.at[e], pair(info_sem), jnp.bitwise_xor(dom, e), tile).start()
+        return carry
+
+    lax.fori_loop(1, 8, small_dom, 0)
+
+    pl.semaphore_wait(all_sem, 7)
+
+    def ship(i, carry):
+        t = jnp.bitwise_xor(tile, turn_of(i))
         for e in range(8):
-            ship(u, e, t)
-        return carry
-
-    lax.fori_loop(1, 16, rows_of, 0)
-    here = pack(0)
-    for e in range(1, 8):
-        ship(0, e, here)
-    rb[0, 0] = sb[0, dom]
+            d = jnp.bitwise_xor(dom, e)
+            remote(sb.at[i, d], rb.at[i, e], (data_send, data_recv.at[i]), d, t).start()
+        return carry
+
+    lax.fori_loop(0, FIRST, ship, 0)
+    lax.fori_loop(EARLY, 16, pack, 0)
+    rb[15, 0] = sb[15, dom]
 
     wait_for(meta1.at[pl.ds(1, 15)], m1_sem.at[1])
     for u in range(16):
@@ -247,7 +273,7 @@
                 xc[pl.ds(at, 16), r * WIDE + 256:(r + 1) * WIDE] = squares[r * 16:(r + 1) * 16]
             return inner
 
-        lax.fori_loop(0, CHUNK // 16, block, 0)
+        lax.fori_loop(0, CHUNK // 16, block, 0, unroll=4)
         score[pl.ds(base, CHUNK), :] = SCALE * lax.dot_general(xc[...], xw[...], NT, preferred_element_type=F32)
 
         def share(v, inner):
@@ -265,6 +291,7 @@
 
     lax.fori_loop(0, 4, scored, 0)
     part[0] = score[pl.ds(pl.multiple_of(tile * 64, 64), 64), :]
+    lax.fori_loop(FIRST, SECOND, ship, 0)
 
     wait_for(info.at[pl.ds(1, 7)], info_sem.at[1])
     wait_for(noise.at[pl.ds(1, 15)], noise_sem.at[1])
@@ -281,7 +308,8 @@
     focus_rows = stack[...].astype(BF16)
     lane2 = iota((1, 256), 1)
 
-    def prepare(u, carry):
+    def prepare(i, carry):
+        u = turn_of(i)
         quarter = lane1 >> 5
         strips, numbers = [], []
         for half in range(2):
@@ -296,11 +324,11 @@
             numbers.append(number)
         strip = jnp.concatenate(strips, axis=1).astype(I32) - 1
         number = jnp.concatenate(numbers, axis=1).astype(I32)
-        low[u] = (strip & 255).astype(F32)
-        high[u] = (strip >> 8).astype(F32)
+        low[i] = (strip & 255).astype(F32)
+        high[i] = (strip >> 8).astype(F32)
         r = number & 15
         particle = ((number >> 4) & 63) + 64 * ((lane2 >> 5) & 1)
-        code[u] = (particle + 128 * (number >> 10)).astype(F32)
+        code[i] = (particle + 128 * (number >> 10)).astype(F32)
         hot = jnp.where(iota((HALF, 256), 0) == particle, 1.0, 0.0).astype(BF16)
         found = jnp.dot(focus_rows, hot, preferred_element_type=F32)
         found = jnp.where((iota((16, 256), 0) >> 2) == (lane2 >> 6), found, 0.0)
@@ -308,7 +336,7 @@
         row_f = freq_sq(jnp.bitwise_xor(tile, u) * 16 + r)
         offset = slope * (row_f * row_f) + PHASE
         which = iota((8, 256), 0)
-        rows = jnp.where(which == 0, slope, jnp.where(which == 1, offset, r.astype(F32)))
+        rows = jnp.where(which == 0, slope, jnp.where(which == 1, offset, jnp.where(which == 2, r.astype(F32), strip.astype(F32))))
         turned = jnp.transpose(rows)
         col_f = iota((256, HALF), 1).astype(F32)
         contrast = wave(turned[:, 0:1] * (col_f * col_f) + turned[:, 1:2])
@@ -318,7 +346,10 @@
         second = (full - first.astype(F32)).astype(BF16)
         third = (full - first.astype(F32) - second.astype(F32)).astype(BF16)
         gain = jnp.dot(pick_row, jnp.concatenate([first, second, third], axis=0), preferred_element_type=F32)
-        pm[u] = (contrast * contrast * gain).astype(BF16)
+        power = contrast * contrast * gain
+        upper_half = turned[:, 3:4] >= 1024.0
+        pm[i, :, 0:HALF] = jnp.where(upper_half, 0.0, power).astype(BF16)
+        pm[i, :, HALF:] = jnp.where(upper_half, power, 0.0).astype(BF16)
         return carry
 
     lax.fori_loop(0, 8, prepare, 0)
@@ -348,6 +379,7 @@
         return carry
 
     lax.fori_loop(1, 32, tell, 0)
+    lax.fori_loop(SECOND, THIRD, ship, 0)
     lax.fori_loop(8, 12, prepare, 0)
     wait_for(stats.at[pl.ds(1, 31)], stat_sem.at[1])
     every = stats[...]
@@ -372,6 +404,14 @@
         return carry
 
     lax.fori_loop(1, 4, pass_on, 0)
+    lax.fori_loop(THIRD, 15, ship, 0)
+
+    def ship_last(e, carry):
+        d = jnp.bitwise_xor(dom, e)
+        remote(sb.at[15, d], rb.at[15, e], (data_send, data_recv.at[15]), d, tile).start()
+        return carry
+
+    lax.fori_loop(1, 8, ship_last, 0)
     lax.fori_loop(12, 16, prepare, 0)
     wait_for(picks.at[pl.ds(1, 3)], pick_sem.at[1])
     for w in range(4):
@@ -388,36 +428,39 @@
 
     lax.fori_loop(0, 16, choose, 0)
 
-    order = [(i * 7) % 16 for i in range(1, 16)]
-    del order
     slab_row = iota((256, 4 * 256), 0).astype(F32).astype(BF16)
     for g in range(4):
-        for u in range(4 * g, 4 * g + 4):
-            if u == 0:
-                wait_for(rb.at[0, pl.ds(0, 7)], data_recv.at[0])
+        for i in range(4 * g, 4 * g + 4):
+            if i == 15:
+                wait_for(rb.at[15, pl.ds(1, 7)], data_recv.at[15])
             else:
-                wait_for(rb.at[u], data_recv.at[u])
-        low16 = jnp.concatenate([low[u] for u in range(4 * g, 4 * g + 4)], axis=1).astype(BF16)
-        high_row = jnp.concatenate([high[u] for u in range(4 * g, 4 * g + 4)], axis=1)
-        share_row = jnp.concatenate([weight[u] for u in range(4 * g, 4 * g + 4)], axis=1)
+                wait_for(rb.at[i], data_recv.at[i])
+        low16 = jnp.concatenate([low[i] for i in range(4 * g, 4 * g + 4)], axis=1).astype(BF16)
+        high_row = jnp.concatenate([high[i] for i in range(4 * g, 4 * g + 4)], axis=1)
+        share_row = jnp.concatenate([weight[i] for i in range(4 * g, 4 * g + 4)], axis=1)
 
         def insert(b, carry):
-            value = jnp.where(high_row == b.astype(F32), share_row, 0.0).astype(BF16)
-            spot = jnp.where(slab_row == low16, value, jnp.zeros_like(value))
+            match = slab_row == low16
             rows = rb[4 * g:4 * g + 4].reshape(1024, 256)
-            power = pm[4 * g:4 * g + 4].reshape(1024, HALF)
-            at = pl.ds(pl.multiple_of(b * 256, 256), 256)
-            data = jnp.dot(spot, rows, preferred_element_type=F32)
-            more = jnp.dot(spot, power, preferred_element_type=F32)
-            if g == 0:
-                vol_ref[at, 0:256] = data
-                vol_ref[at, 256:] = more
-            else:
-                vol_ref[at, 0:256] += data
-                vol_ref[at, 256:] += more
+            power = pm[4 * g:4 * g + 4].reshape(1024, 256)
+            spots = []
+            for h in range(2):
+                value = jnp.where(high_row == (b + 4 * h).astype(F32), share_row, 0.0).astype(BF16)
+                spots.append(jnp.where(match, value, jnp.zeros_like(value)))
+            both = jnp.dot(spots[0] + spots[1], power, preferred_element_type=F32)
+            for h in range(2):
+                at = pl.ds(pl.multiple_of((b + 4 * h) * 256, 256), 256)
+                data = jnp.dot(spots[h], rows, preferred_element_type=F32)
+                more = both[:, h * HALF:(h + 1) * HALF]
+                if g == 0:
+                    vol_ref[at, 0:256] = data
+                    vol_ref[at, 256:] = more
+                else:
+                    vol_ref[at, 0:256] += data
+                    vol_ref[at, 256:] += more
             return carry
 
-        lax.fori_loop(0, 8, insert, 0)
+        lax.fori_loop(0, 4, insert, 0)
 
     wait_for(xw.at[mine], xw_sem.at[0])
     wait_for(meta1.at[pl.ds(1, 15)], m1_sem.at[0])
@@ -427,18 +470,14 @@
     wait_for(part.at[pl.ds(1, 15)], part_sem.at[0])
     wait_for(stats.at[pl.ds(1, 31)], stat_sem.at[0])
     wait_for(picks.at[pl.ds(1, 3)], pick_sem.at[0])
-    wait_for(sb.at[pl.ds(1, 15)], data_send)
-    wait_for(sb.at[0, pl.ds(0, 7)], data_send)
+    wait_for(sb.at[pl.ds(0, 15)], data_send)
+    wait_for(sb.at[15, pl.ds(0, 7)], data_send)
 
 
 def shards(images, defocus, noise_weight, references, candidates, route, strips):
     rows = images.reshape(MINE, 2 * HALF)
-    focus = jnp.broadcast_to(defocus[:, None, None], (PD, 1, HALF))
-    cand = jnp.transpose(candidates).astype(F32)
-    short = jnp.concatenate([cand, defocus[None], jnp.zeros((5, PD), F32)], axis=0)
-    info = jnp.concatenate([short, short], axis=1)
-    owners = jnp.transpose(route[0, 0], (1, 0, 2)).reshape(2, MINE)
-    places = jnp.transpose(strips[0, 0], (1, 0, 2)).reshape(2, MINE)
+    focus = defocus[None]
+    turned = [jnp.transpose(x[0, 0], (1, 2, 0)) for x in (route, strips)]
     vmem = pl.BlockSpec(memory_space=pltpu.VMEM)
     dma = pltpu.SemaphoreType.DMA
     volume, spread = pl.pallas_call(
@@ -463,6 +502,7 @@
             pltpu.VMEM((16, 8, 1, HALF), F32),
             pltpu.VMEM((16, 8, 1, HALF), F32),
             pltpu.VMEM((8, 16, 1, HALF), F32),
+            pltpu.VMEM((8, MINE), F32),
             pltpu.VMEM((8, 8, HALF), F32),
             pltpu.VMEM((16, 16, HALF), F32),
             pltpu.VMEM((REFS, 2 * PD), F32),
@@ -475,15 +515,16 @@
             pltpu.VMEM((16, 1, 256), F32),
             pltpu.VMEM((16, 1, 256), F32),
             pltpu.VMEM((16, 1, 256), F32),
-            pltpu.VMEM((16, 256, HALF), BF16),
+            pltpu.VMEM((16, 256, 256), BF16),
             dma((REFS // CHUNK,)),
             dma,
             dma((16,)),
+            pltpu.SemaphoreType.REGULAR,
         ] + [dma((2,))] * 8,
         compiler_params=pltpu.CompilerParams(
             collective_id=0, has_side_effects=True, vmem_limit_bytes=56 << 20
         ),
-    )(rows, focus, info, noise_weight, references, owners, places)
+    )(rows, focus, candidates.T, noise_weight, references, *turned)
     return volume, spread[2, :PD]
 
 

time: 91.3 us -> 70.5 us (0.77)
  Pallas kernels: 78.9 us -> 64.7 us
  local copies, waits for them, and re-layouts: 9.33 us -> 4.94 us
  other arithmetic: 2.08 us -> 0 us
    pallas_call x1, Pallas kernels: 78.9 us -> 64.7 us  [shards(): pl.pallas_call(kernel, out_shape=(jax.ShapeDtypeStruct((STRIPS, WIDE), F3...]
    transpose x2 -> x0, local copies, waits for them, and re-layouts: 1.6 us -> none  [the longest x1 0.8 us: shards(): owners = jnp.transpose(route[0, 0], (1, 0, 2)).reshape(2, MINE)]
    broadcast_in_dim x2 -> x0, local copies, waits for them, and re-layouts: 1.4 us -> none  [the longest x1 1.4 us: shards(): focus = jnp.broadcast_to(defocus[:, None, None], (PD, 1, HALF))]
    concatenate x1 -> x0, other arithmetic: 1.4 us -> none  [shards(): info = jnp.concatenate([short, short], axis=1)]
    reshape x2 -> x0, local copies, waits for them, and re-layouts: 1.38 us -> none  [the longest x1 0.7 us: shards(): places = jnp.transpose(strips[0, 0], (1, 0, 2)).reshape(2, MINE)]
where the time goes in v2:
time: 70.5 us; the launch traced here: 70.3 us
  Pallas kernels  64.7 us (92%)
  local copies, waits for them, and re-layouts  4.94 us (7%)
    pallas_call x1, Pallas kernels, shards(): pl.pallas_call(kernel, out_shape=(jax.ShapeDtypeStruct((STRIPS, WIDE), F3...  64.7 us
    unnamed x1, local copies, waits for them, and re-layouts  3.75 us

profile of v2, /device:TPU:1, one launch (start us, length us, event | category | flops | bytes accessed | tf_op | source)
XLA Modules:
  0.0 70.3 jit_solution(3573883597602032545)
XLA Ops:
  0.6 64.7 %shard_map.86 = (f32[2048,384]{1,0:T(8,128)}, f32[8,128]{1,0:T(8,128)}) custom-call(bf16[1024,256]{1,0:T(8,128)(2,1)} %bitcast.11, f32[1,64]{1,0:T(1,128)} %bitcast.15, s32[2,64]{1,0:T(2,128)} %bitcast.14, f32[16,128]{1,0:T(8,128)} %noise_ref.1, bf16[2048,16,256]{2,1,0:T(8,128)(2,1)} %refs_ref.1, s32[2,16,64]{2,1,0:T(8,128)} %bitcast.12, s32[2,16,64]{2,1,0:T(8,128)} %bitcast.13), custom_call_target="tpu_custom_call" | custom-call | tf_op jit(solution)/shard_map/pallas_call | solution.py:483
  65.3 1.2 %slice_bitcast_fusion = f32[64]{0:T(128)} fusion(f32[8,128]{1,0:T(8,128)} %get-tuple-element.5), kind=kLoop, calls=%fused_computation | loop fusion | bytes 512 | tf_op jit(solution)/shard_map/squeeze | solution.py:528
  66.5 3.8 %copy.10 = f32[2048,384]{1,0:T(8,128)} copy(f32[2048,384]{1,0:T(8,128)} %get-tuple-element.8) | data formatting | bytes 6291456

commit v3 on v2

--- a/solution.py
+++ b/solution.py
@@ -23,8 +23,8 @@
 WIDE = 3 * HALF
 DEPTH = ROWS_DEV * WIDE
 CHUNK = 256
-EARLY = 8
-FIRST, SECOND, THIRD = 8, 11, 14
+FIRST, SECOND, THIRD = 6, 8, 11
+SHIFT = (0, 5, 10, 15, 3, 6, 9, 12)
 
 TURN = 400.0 / 65536.0 / (2.0 * math.pi)
 PHASE = 0.1 / (2.0 * math.pi)
@@ -152,6 +152,27 @@
         for i in range(16):
             xw[pl.ds(at, 16), i * WIDE:i * WIDE + 256] = left[i * 16:(i + 1) * 16]
             xw[pl.ds(at, 16), i * WIDE + 256:(i + 1) * WIDE] = right[i * 16:(i + 1) * 16]
+
+    pl.semaphore_wait(barrier, 22)
+    lax.fori_loop(1, 8, vouch, 0)
+    mate = jnp.bitwise_xor(dom, 1)
+    mine = pl.ds(pl.multiple_of(core * PD, PD), PD)
+    other = pl.ds(pl.multiple_of((1 - core) * PD, PD), PD)
+    remote(xw.at[mine], xw.at[mine], pair(xw_sem), mate, tile).start()
+    noise[0] = noise_ref[...]
+
+    def small(u, carry):
+        t = jnp.bitwise_xor(tile, u)
+        remote(noise_ref, noise.at[u], pair(noise_sem), dom, t).start()
+        return carry
+
+    lax.fori_loop(1, 16, small, 0)
+
+    def small_dom(e, carry):
+        remote(info.at[0], info.at[e], pair(info_sem), jnp.bitwise_xor(dom, e), tile).start()
+        return carry
+
+    lax.fori_loop(1, 8, small_dom, 0)
 
     upper = jnp.where(ia < ib, 1.0, 0.0).astype(BF16)
     running = jnp.zeros((128, 1), F32)
@@ -188,58 +209,45 @@
     for k in range(2):
         mask_ref[k] = jnp.where(slot_id == rank_ref[k:k + 1, :], 1.0, 0.0).astype(BF16)
 
+    meta1[0] = meta0[tile]
+
+    def small_meta(u, carry):
+        t = jnp.bitwise_xor(tile, u)
+        remote(meta0.at[t], meta1.at[u], pair(m1_sem), dom, t).start()
+        return carry
+
+    lax.fori_loop(1, 16, small_meta, 0)
+
     def turn_of(i):
         return lax.rem(7 * (i + 1), 16)
 
     def pack(i, carry):
-        t = jnp.bitwise_xor(tile, turn_of(i))
         blocks = []
-        for d in range(8):
-            one = ot[0, t, d:d + 1, :].astype(BF16)
-            two = ot[1, t, d:d + 1, :].astype(BF16)
+        for e in range(8):
+            t = jnp.bitwise_xor(tile, jnp.bitwise_xor(turn_of(i), SHIFT[e]))
+            d = pl.ds(jnp.bitwise_xor(dom, e), 1)
+            one = ot[0, t, d, :].astype(BF16)
+            two = ot[1, t, d, :].astype(BF16)
             blocks.append(mask_ref[0] * one + mask_ref[1] * two)
         rows = jnp.dot(jnp.concatenate(blocks, axis=0), wi[...], preferred_element_type=F32).astype(BF16)
-        for d in range(8):
-            sb[i, d] = rows[d * 32:(d + 1) * 32]
-        return carry
-
-    lax.fori_loop(0, EARLY, pack, 0)
-
-    pl.semaphore_wait(barrier, 22)
-    lax.fori_loop(1, 8, vouch, 0)
-    mate = jnp.bitwise_xor(dom, 1)
-    mine = pl.ds(pl.multiple_of(core * PD, PD), PD)
-    other = pl.ds(pl.multiple_of((1 - core) * PD, PD), PD)
-    remote(xw.at[mine], xw.at[mine], pair(xw_sem), mate, tile).start()
-    meta1[0] = meta0[tile]
-    noise[0] = noise_ref[...]
-
-    def small(u, carry):
-        t = jnp.bitwise_xor(tile, u)
-        remote(meta0.at[t], meta1.at[u], pair(m1_sem), dom, t).start()
-        remote(noise_ref, noise.at[u], pair(noise_sem), dom, t).start()
-        return carry
-
-    lax.fori_loop(1, 16, small, 0)
-
-    def small_dom(e, carry):
-        remote(info.at[0], info.at[e], pair(info_sem), jnp.bitwise_xor(dom, e), tile).start()
-        return carry
-
-    lax.fori_loop(1, 8, small_dom, 0)
+        for e in range(8):
+            sb[i, e] = rows[e * 32:(e + 1) * 32]
+        return carry
 
     pl.semaphore_wait(all_sem, 7)
 
     def ship(i, carry):
-        t = jnp.bitwise_xor(tile, turn_of(i))
         for e in range(8):
+            t = jnp.bitwise_xor(tile, jnp.bitwise_xor(turn_of(i), SHIFT[e]))
             d = jnp.bitwise_xor(dom, e)
-            remote(sb.at[i, d], rb.at[i, e], (data_send, data_recv.at[i]), d, t).start()
-        return carry
-
-    lax.fori_loop(0, FIRST, ship, 0)
-    lax.fori_loop(EARLY, 16, pack, 0)
-    rb[15, 0] = sb[15, dom]
+            remote(sb.at[i, e], rb.at[i, e], (data_send, data_recv.at[i]), d, t).start()
+        return carry
+
+    def pack_ship(i, carry):
+        pack(i, 0)
+        return ship(i, 0)
+
+    lax.fori_loop(0, FIRST, pack_ship, 0)
 
     wait_for(meta1.at[pl.ds(1, 15)], m1_sem.at[1])
     for u in range(16):
@@ -273,7 +281,7 @@
                 xc[pl.ds(at, 16), r * WIDE + 256:(r + 1) * WIDE] = squares[r * 16:(r + 1) * 16]
             return inner
 
-        lax.fori_loop(0, CHUNK // 16, block, 0, unroll=4)
+        lax.fori_loop(0, CHUNK // 16, block, 0, unroll=8)
         score[pl.ds(base, CHUNK), :] = SCALE * lax.dot_general(xc[...], xw[...], NT, preferred_element_type=F32)
 
         def share(v, inner):
@@ -291,7 +299,7 @@
 
     lax.fori_loop(0, 4, scored, 0)
     part[0] = score[pl.ds(pl.multiple_of(tile * 64, 64), 64), :]
-    lax.fori_loop(FIRST, SECOND, ship, 0)
+    lax.fori_loop(FIRST, SECOND, pack_ship, 0)
 
     wait_for(info.at[pl.ds(1, 7)], info_sem.at[1])
     wait_for(noise.at[pl.ds(1, 15)], noise_sem.at[1])
@@ -316,7 +324,8 @@
             strip = jnp.zeros((1, HALF), F32)
             number = jnp.zeros((1, HALF), F32)
             for a in range(4):
-                got = meta2[half * 4 + a, u]
+                e = half * 4 + a
+                got = meta2[e, jnp.bitwise_xor(u, SHIFT[e])]
                 back = pltpu.roll(got, 64, 1)
                 strip = jnp.where(quarter == a, got if a < 2 else back, strip)
                 number = jnp.where(quarter == a, back if a < 2 else got, number)
@@ -333,15 +342,18 @@
         found = jnp.dot(focus_rows, hot, preferred_element_type=F32)
         found = jnp.where((iota((16, 256), 0) >> 2) == (lane2 >> 6), found, 0.0)
         slope = jnp.sum(found, axis=0, keepdims=True) * TURN
-        row_f = freq_sq(jnp.bitwise_xor(tile, u) * 16 + r)
+        source = lane2 >> 5
+        shift = ((source & 1) * 5) ^ (((source >> 1) & 1) * 10) ^ ((source >> 2) * 3)
+        row_f = freq_sq((shift ^ jnp.bitwise_xor(tile, u)) * 16 + r)
         offset = slope * (row_f * row_f) + PHASE
         which = iota((8, 256), 0)
-        rows = jnp.where(which == 0, slope, jnp.where(which == 1, offset, jnp.where(which == 2, r.astype(F32), strip.astype(F32))))
+        rows = jnp.where(which == 0, slope, jnp.where(which == 1, offset, jnp.where(which == 2, (r + 16 * source).astype(F32), strip.astype(F32))))
         turned = jnp.transpose(rows)
         col_f = iota((256, HALF), 1).astype(F32)
         contrast = wave(turned[:, 0:1] * (col_f * col_f) + turned[:, 1:2])
-        pick_row = jnp.where((iota((256, 48), 1) & 15).astype(F32) == turned[:, 2:3], 1.0, 0.0).astype(BF16)
-        full = noise[u]
+        pick_row = jnp.where(iota((256, HALF), 1).astype(F32) == turned[:, 2:3], 1.0, 0.0).astype(BF16)
+        pick_row = jnp.concatenate([pick_row] * 3, axis=1)
+        full = jnp.concatenate([noise[jnp.bitwise_xor(u, SHIFT[e])] for e in range(8)], axis=0)
         first = full.astype(BF16)
         second = (full - first.astype(F32)).astype(BF16)
         third = (full - first.astype(F32) - second.astype(F32)).astype(BF16)
@@ -379,7 +391,7 @@
         return carry
 
     lax.fori_loop(1, 32, tell, 0)
-    lax.fori_loop(SECOND, THIRD, ship, 0)
+    lax.fori_loop(SECOND, THIRD, pack_ship, 0)
     lax.fori_loop(8, 12, prepare, 0)
     wait_for(stats.at[pl.ds(1, 31)], stat_sem.at[1])
     every = stats[...]
@@ -404,14 +416,13 @@
         return carry
 
     lax.fori_loop(1, 4, pass_on, 0)
-    lax.fori_loop(THIRD, 15, ship, 0)
-
-    def ship_last(e, carry):
-        d = jnp.bitwise_xor(dom, e)
-        remote(sb.at[15, d], rb.at[15, e], (data_send, data_recv.at[15]), d, tile).start()
-        return carry
-
-    lax.fori_loop(1, 8, ship_last, 0)
+    lax.fori_loop(THIRD, 15, pack_ship, 0)
+    pack(15, 0)
+    rb[15, 0] = sb[15, 0]
+
+    for e in range(1, 8):
+        t = jnp.bitwise_xor(tile, SHIFT[e])
+        remote(sb.at[15, e], rb.at[15, e], (data_send, data_recv.at[15]), jnp.bitwise_xor(dom, e), t).start()
     lax.fori_loop(12, 16, prepare, 0)
     wait_for(picks.at[pl.ds(1, 3)], pick_sem.at[1])
     for w in range(4):
@@ -471,7 +482,7 @@
     wait_for(stats.at[pl.ds(1, 31)], stat_sem.at[0])
     wait_for(picks.at[pl.ds(1, 3)], pick_sem.at[0])
     wait_for(sb.at[pl.ds(0, 15)], data_send)
-    wait_for(sb.at[15, pl.ds(0, 7)], data_send)
+    wait_for(sb.at[15, pl.ds(1, 7)], data_send)
 
 
 def shards(images, defocus, noise_weight, references, candidates, route, strips):

time: 70.5 us -> 61.9 us (0.88)
  Pallas kernels: 64.7 us -> 56.1 us
    pallas_call x1, Pallas kernels: 64.7 us -> 56.1 us  [shards(): pl.pallas_call(kernel, out_shape=(jax.ShapeDtypeStruct((STRIPS, WIDE), F3...]
where the time goes in v3:
time: 61.9 us; the launch traced here: 61.7 us
  Pallas kernels  56.1 us (91%)
  local copies, waits for them, and re-layouts  4.94 us (8%)
  between operations  0.64 us (1%)
    pallas_call x1, Pallas kernels, shards(): pl.pallas_call(kernel, out_shape=(jax.ShapeDtypeStruct((STRIPS, WIDE), F3...  56.1 us
    unnamed x1, local copies, waits for them, and re-layouts  3.75 us

profile of v3, /device:TPU:1, one launch (start us, length us, event | category | flops | bytes accessed | tf_op | source)
XLA Modules:
  0.0 61.7 jit_solution(13528028097139686717)
XLA Ops:
  0.6 56.1 %shard_map.86 = (f32[2048,384]{1,0:T(8,128)}, f32[8,128]{1,0:T(8,128)}) custom-call(bf16[1024,256]{1,0:T(8,128)(2,1)} %bitcast.11, f32[1,64]{1,0:T(1,128)} %bitcast.15, s32[2,64]{1,0:T(2,128)} %bitcast.14, f32[16,128]{1,0:T(8,128)} %noise_ref.1, bf16[2048,16,256]{2,1,0:T(8,128)(2,1)} %refs_ref.1, s32[2,16,64]{2,1,0:T(8,128)} %bitcast.12, s32[2,16,64]{2,1,0:T(8,128)} %bitcast.13), custom_call_target="tpu_custom_call" | custom-call | tf_op jit(solution)/shard_map/pallas_call | solution.py:494
  56.7 1.2 %slice_bitcast_fusion = f32[64]{0:T(128)} fusion(f32[8,128]{1,0:T(8,128)} %get-tuple-element.5), kind=kLoop, calls=%fused_computation | loop fusion | bytes 512 | tf_op jit(solution)/shard_map/squeeze | solution.py:539
  57.9 3.8 %copy.10 = f32[2048,384]{1,0:T(8,128)} copy(f32[2048,384]{1,0:T(8,128)} %get-tuple-element.8) | data formatting | bytes 6291456

commit v4 on v3

--- a/solution.py
+++ b/solution.py
@@ -54,7 +54,7 @@
 
 def kernel(
     img_ref, focus_ref, cand_ref, noise_ref, refs_ref, route_ref, place_ref,
-    vol_ref, spread_ref,
+    vol_ref, rows_ref, power_ref, label_ref, spread_ref,
     rv, xc, xw, wi, pmo, ot, rank_ref, mask_ref, sb, rb, meta0, meta1, meta2,
     lanes, info, noise, score, part, stats, picks, stack, table, low, high, code, weight, pm,
     ref_sem, data_send, data_recv, all_sem, xw_sem, info_sem, noise_sem, m1_sem, m2_sem, part_sem, stat_sem, pick_sem,
@@ -446,9 +446,17 @@
                 wait_for(rb.at[15, pl.ds(1, 7)], data_recv.at[15])
             else:
                 wait_for(rb.at[i], data_recv.at[i])
-        low16 = jnp.concatenate([low[i] for i in range(4 * g, 4 * g + 4)], axis=1).astype(BF16)
+        low_row = jnp.concatenate([low[i] for i in range(4 * g, 4 * g + 4)], axis=1)
         high_row = jnp.concatenate([high[i] for i in range(4 * g, 4 * g + 4)], axis=1)
         share_row = jnp.concatenate([weight[i] for i in range(4 * g, 4 * g + 4)], axis=1)
+        if g == 3:
+            rows_ref[...] = rb[12:16].reshape(1024, 256)
+            power_ref[...] = pm[12:16].reshape(1024, 256)
+            label_ref[0:1, :] = low_row
+            label_ref[1:2, :] = high_row
+            label_ref[2:3, :] = share_row
+            break
+        low16 = low_row.astype(BF16)
 
         def insert(b, carry):
             match = slab_row == low16
@@ -485,20 +493,38 @@
     wait_for(sb.at[15, pl.ds(1, 7)], data_send)
 
 
+def finish(part_ref, rows_ref, power_ref, label_ref, stat_ref, vol_ref, spread_ref):
+    b = pl.program_id(0)
+    match = iota((256, 1024), 0).astype(F32).astype(BF16) == label_ref[0:1, :].astype(BF16)
+    spots = []
+    for h in range(2):
+        value = jnp.where(label_ref[1:2, :] == (b + 4 * h).astype(F32), label_ref[2:3, :], 0.0).astype(BF16)
+        spots.append(jnp.where(match, value, jnp.zeros_like(value)))
+    both = jnp.dot(spots[0] + spots[1], power_ref[...], preferred_element_type=F32)
+    for h in range(2):
+        data = jnp.dot(spots[h], rows_ref[...], preferred_element_type=F32)
+        vol_ref[h, :, 0:256] = part_ref[h, :, 0:256] + data
+        vol_ref[h, :, 256:] = part_ref[h, :, 256:] + both[:, h * HALF:(h + 1) * HALF]
+    spread_ref[...] = stat_ref[2:3, 0:PD]
+
+
 def shards(images, defocus, noise_weight, references, candidates, route, strips):
     rows = images.reshape(MINE, 2 * HALF)
     focus = defocus[None]
     turned = [jnp.transpose(x[0, 0], (1, 2, 0)) for x in (route, strips)]
     vmem = pl.BlockSpec(memory_space=pltpu.VMEM)
     dma = pltpu.SemaphoreType.DMA
-    volume, spread = pl.pallas_call(
+    partial, last_rows, last_power, labels, stat = pl.pallas_call(
         kernel,
         out_shape=(
             jax.ShapeDtypeStruct((STRIPS, WIDE), F32),
+            jax.ShapeDtypeStruct((1024, 256), BF16),
+            jax.ShapeDtypeStruct((1024, 256), BF16),
+            jax.ShapeDtypeStruct((8, 1024), F32),
             jax.ShapeDtypeStruct((8, HALF), F32),
         ),
         in_specs=[vmem, vmem, vmem, vmem, pl.BlockSpec(memory_space=pl.ANY), vmem, vmem],
-        out_specs=(vmem, vmem),
+        out_specs=(vmem,) * 5,
         scratch_shapes=[
             pltpu.VMEM((REFS, ROWS_DEV, 2 * HALF), BF16),
             pltpu.VMEM((CHUNK, DEPTH), BF16),
@@ -536,7 +562,23 @@
             collective_id=0, has_side_effects=True, vmem_limit_bytes=56 << 20
         ),
     )(rows, focus, candidates.T, noise_weight, references, *turned)
-    return volume, spread[2, :PD]
+    half = pl.BlockSpec((2, 256, WIDE), lambda b: (0, b, 0))
+
+    def whole(shape):
+        return pl.BlockSpec(shape, lambda b: (0, 0))
+
+    volume, spread = pl.pallas_call(
+        finish,
+        grid=(4,),
+        out_shape=(
+            jax.ShapeDtypeStruct((2, STRIPS // 2, WIDE), F32),
+            jax.ShapeDtypeStruct((1, PD), F32),
+        ),
+        in_specs=[half, whole((1024, 256)), whole((1024, 256)), whole((8, 1024)), whole((8, HALF))],
+        out_specs=(half, whole((1, PD))),
+        compiler_params=pltpu.CompilerParams(vmem_limit_bytes=62 << 20),
+    )(partial.reshape(2, STRIPS // 2, WIDE), last_rows, last_power, labels, stat)
+    return volume.reshape(STRIPS, WIDE), spread[0]
 
 
 def solution(mesh):

time: 61.9 us -> 60.4 us (0.976)
  local copies, waits for them, and re-layouts: 4.94 us -> 0 us
  Pallas kernels: 56.1 us -> 59.6 us
    pallas_call x0 -> x1, Pallas kernels: none -> 5.6 us  [shards(): pl.pallas_call(finish, grid=(4,), out_shape=(jax.ShapeDtypeStruct((2, STR...]
    unnamed x1 -> x0, local copies, waits for them, and re-layouts: 3.75 us -> none
    pallas_call x1, Pallas kernels: 56.1 us -> 54 us  [shards(): pl.pallas_call(kernel, out_shape=(jax.ShapeDtypeStruct((STRIPS, WIDE), F3...]
    squeeze x1 -> x0, local copies, waits for them, and re-layouts: 1.19 us -> none  [shards(): return (volume, spread[2, :PD])]
where the time goes in v4:
time: 60.4 us; the launch traced here: 60.2 us
  Pallas kernels  59.6 us (99%)
  between operations  0.64 us (1%)
    pallas_call x1, Pallas kernels, shards(): pl.pallas_call(kernel, out_shape=(jax.ShapeDtypeStruct((STRIPS, WIDE), F3...  54 us
    pallas_call x1, Pallas kernels, shards(): pl.pallas_call(finish, grid=(4,), out_shape=(jax.ShapeDtypeStruct((2, STR...  5.6 us

profile of v4, /device:TPU:1, one launch (start us, length us, event | category | flops | bytes accessed | tf_op | source)
XLA Modules:
  0.0 60.2 jit_solution(11665207493744295948)
XLA Ops:
  0.6 54.0 %shard_map.86 = (f32[2048,384]{1,0:T(8,128)}, bf16[1024,256]{1,0:T(8,128)(2,1)}, bf16[1024,256]{1,0:T(8,128)(2,1)}, f32[8,1024]{1,0:T(8,128)}, f32[8,128]{1,0:T(8,128)}) custom-call(bf16[1024,256]{1,0:T(8,128)(2,1)} %bitcast.13, f32[1,64]{1,0:T(1,128)} %bitcast.17, s32[2,64]{1,0:T(2,128)} %bitcast.16, f32[16,128]{1,0:T(8,128)} %noise_ref.1, ...), custom_call_target="tpu_custom_call" | custom-call | tf_op jit(solution)/shard_map/pallas_call | solution.py:517
  54.6 5.6 %shard_map.87 = (f32[2,1024,384]{2,1,0:T(8,128)}, f32[1,64]{1,0:T(1,128)}) custom-call(f32[2,1024,384]{2,1,0:T(8,128)} %bitcast.12, bf16[1024,256]{1,0:T(8,128)(2,1)} %get-tuple-element.10.rows_ref, bf16[1024,256]{1,0:T(8,128)(2,1)} %get-tuple-element.11.power_ref, f32[8,1024]{1,0:T(8,128)} %get-tuple-element.12.label_ref, f32[8,128]{1,0:T(8,128)} %get-tuple-element.13.stat_ref), custom_call_target="tpu_custom_call" | custom-call | tf_op jit(solution)/shard_map/pallas_call | solution.py:570

commit v5 on v4

--- a/solution.py
+++ b/solution.py
@@ -437,7 +437,7 @@
         weight[u] = jnp.sum(jnp.where(keep, found, 0.0), axis=0, keepdims=True)
         return carry
 
-    lax.fori_loop(0, 16, choose, 0)
+    lax.fori_loop(0, 16, choose, 0, unroll=8)
 
     slab_row = iota((256, 4 * 256), 0).astype(F32).astype(BF16)
     for g in range(4):

time: 60.4 us -> 58.9 us (0.975)
  Pallas kernels: 59.6 us -> 58.1 us
    pallas_call x1, Pallas kernels: 54 us -> 52.5 us  [shards(): pl.pallas_call(kernel, out_shape=(jax.ShapeDtypeStruct((STRIPS, WIDE), F3...]
where the time goes in v5:
time: 58.9 us; the launch traced here: 58.7 us
  Pallas kernels  58.1 us (99%)
  between operations  0.64 us (1%)
    pallas_call x1, Pallas kernels, shards(): pl.pallas_call(kernel, out_shape=(jax.ShapeDtypeStruct((STRIPS, WIDE), F3...  52.5 us
    pallas_call x1, Pallas kernels, shards(): pl.pallas_call(finish, grid=(4,), out_shape=(jax.ShapeDtypeStruct((2, STR...  5.61 us

profile of v5, /device:TPU:1, one launch (start us, length us, event | category | flops | bytes accessed | tf_op | source)
XLA Modules:
  0.0 58.7 jit_solution(3623444074508384864)
XLA Ops:
  0.6 52.5 %shard_map.86 = (f32[2048,384]{1,0:T(8,128)}, bf16[1024,256]{1,0:T(8,128)(2,1)}, bf16[1024,256]{1,0:T(8,128)(2,1)}, f32[8,1024]{1,0:T(8,128)}, f32[8,128]{1,0:T(8,128)}) custom-call(bf16[1024,256]{1,0:T(8,128)(2,1)} %bitcast.13, f32[1,64]{1,0:T(1,128)} %bitcast.17, s32[2,64]{1,0:T(2,128)} %bitcast.16, f32[16,128]{1,0:T(8,128)} %noise_ref.1, ...), custom_call_target="tpu_custom_call" | custom-call | tf_op jit(solution)/shard_map/pallas_call | solution.py:517
  53.1 5.6 %shard_map.87 = (f32[2,1024,384]{2,1,0:T(8,128)}, f32[1,64]{1,0:T(1,128)}) custom-call(f32[2,1024,384]{2,1,0:T(8,128)} %bitcast.12, bf16[1024,256]{1,0:T(8,128)(2,1)} %get-tuple-element.10.rows_ref, bf16[1024,256]{1,0:T(8,128)(2,1)} %get-tuple-element.11.power_ref, f32[8,1024]{1,0:T(8,128)} %get-tuple-element.12.label_ref, f32[8,128]{1,0:T(8,128)} %get-tuple-element.13.stat_ref), custom_call_target="tpu_custom_call" | custom-call | tf_op jit(solution)/shard_map/pallas_call | solution.py:570

commit v6 on v5

--- a/solution.py
+++ b/solution.py
@@ -390,7 +390,7 @@
         remote(stats.at[0], stats.at[v], pair(stat_sem), d, t).start()
         return carry
 
-    lax.fori_loop(1, 32, tell, 0)
+    lax.fori_loop(1, 32, tell, 0, unroll=True)
     lax.fori_loop(SECOND, THIRD, pack_ship, 0)
     lax.fori_loop(8, 12, prepare, 0)
     wait_for(stats.at[pl.ds(1, 31)], stat_sem.at[1])
@@ -415,7 +415,7 @@
         remote(picks.at[0], picks.at[w], pair(pick_sem), jnp.bitwise_xor(dom, 2 * w), tile).start()
         return carry
 
-    lax.fori_loop(1, 4, pass_on, 0)
+    lax.fori_loop(1, 4, pass_on, 0, unroll=True)
     lax.fori_loop(THIRD, 15, pack_ship, 0)
     pack(15, 0)
     rb[15, 0] = sb[15, 0]

time: 58.9 us -> 59.1 us (level)
  no operation moved by 1% of the time
where the time goes in v6:
time: 59.1 us; the launch traced here: 58.8 us
  Pallas kernels  58.2 us (98%)
  between operations  0.64 us (1%)
    pallas_call x1, Pallas kernels, shards(): pl.pallas_call(kernel, out_shape=(jax.ShapeDtypeStruct((STRIPS, WIDE), F3...  52.6 us
    pallas_call x1, Pallas kernels, shards(): pl.pallas_call(finish, grid=(4,), out_shape=(jax.ShapeDtypeStruct((2, STR...  5.61 us

profile of v6, /device:TPU:1, one launch (start us, length us, event | category | flops | bytes accessed | tf_op | source)
XLA Modules:
  0.0 58.8 jit_solution(9359746913465387461)
XLA Ops:
  0.6 52.6 %shard_map.86 = (f32[2048,384]{1,0:T(8,128)}, bf16[1024,256]{1,0:T(8,128)(2,1)}, bf16[1024,256]{1,0:T(8,128)(2,1)}, f32[8,1024]{1,0:T(8,128)}, f32[8,128]{1,0:T(8,128)}) custom-call(bf16[1024,256]{1,0:T(8,128)(2,1)} %bitcast.13, f32[1,64]{1,0:T(1,128)} %bitcast.17, s32[2,64]{1,0:T(2,128)} %bitcast.16, f32[16,128]{1,0:T(8,128)} %noise_ref.1, ...), custom_call_target="tpu_custom_call" | custom-call | tf_op jit(solution)/shard_map/pallas_call | solution.py:517
  53.2 5.6 %shard_map.87 = (f32[2,1024,384]{2,1,0:T(8,128)}, f32[1,64]{1,0:T(1,128)}) custom-call(f32[2,1024,384]{2,1,0:T(8,128)} %bitcast.12, bf16[1024,256]{1,0:T(8,128)(2,1)} %get-tuple-element.10.rows_ref, bf16[1024,256]{1,0:T(8,128)(2,1)} %get-tuple-element.11.power_ref, f32[8,1024]{1,0:T(8,128)} %get-tuple-element.12.label_ref, f32[8,128]{1,0:T(8,128)} %get-tuple-element.13.stat_ref), custom_call_target="tpu_custom_call" | custom-call | tf_op jit(solution)/shard_map/pallas_call | solution.py:570
